TPU v7x, 128 devices: a whole 4x4x4 slice. The times are simulated.
128 devices in a mesh: tm: 32 (over z, y, x_lo), slab: 4 (over x_hi, core).
Axes of the slice: x: 4 (x_hi: 2, x_lo: 2; x = x_hi * 2 + x_lo), y: 4, z: 4, core: 2. Of those that a mesh axis runs over, the one named last changes fastest.
Arguments:
- kspace: bfloat16 [2, 64, 4, 96, 9984], P(None, 'tm', None, 'slab'), may hold values from -40 to 40, as said below
- sens: float32 [2, 4, 8, 104, 96], P(None, None, None, 'slab'), may hold values from -3 to 3
Outputs:
- projected: float32 [64, 2, 8, 104, 96], P('tm', None, None, 'slab')
Inputs may be any that keep to these rules, and one draw needn't show every extreme that they name: `kspace`: k-space values of order one with frames of different scale.
All inputs are finite; a program needn't handle non-finite values.
Results may differ from a plain program's by a relative error of at most 0.0036.
Values may be sent and summed in bfloat16 or wider, within the bound.
A program may use at most 128 MiB of HBM per device.

v0:
```python
import jax
import jax.numpy as jnp
from jax import lax
from jax.sharding import PartitionSpec as P

NX = 96
NY = 104
NZ = 96
RANK = 32
ITERS = 4
XW = 8


def inverse_table(length, count, offset):
    outputs = jnp.arange(count, dtype=jnp.int32) + offset
    inputs = jnp.arange(length, dtype=jnp.int32)
    phase = outputs[:, None] * inputs[None, :] % length
    angle = phase.astype(jnp.float32) * (2.0 * jnp.pi / length)
    norm_factor = 1.0 / jnp.sqrt(jnp.float32(length))
    return (jnp.cos(angle) * norm_factor, jnp.sin(angle) * norm_factor)


def contract(pattern, matrix_table, operand):
    return jnp.einsum(pattern, matrix_table, operand, precision=lax.Precision.HIGHEST)


def matmul(left, right):
    return jnp.dot(left, right, precision=lax.Precision.HIGHEST)


def orthonormal(rows, gram):
    factor = jnp.linalg.cholesky(matmul(matmul(rows, gram), rows.T))
    return lax.linalg.triangular_solve(factor, rows, left_side=True, lower=True)


def local(kspace, sens):
    frames_dev = kspace.shape[1]
    coil_count = kspace.shape[2]
    depth_dev = kspace.shape[3]
    spectrum = kspace.astype(jnp.float32).reshape(2, frames_dev, coil_count, depth_dev, NX, NY)
    across_cos, across_sin = inverse_table(NX, XW, (NX - XW) // 2)
    down_cos, down_sin = inverse_table(NY, NY, 0)
    depth_cos, depth_sin = inverse_table(NZ, NZ, 0)
    across_real = contract("jx,fczxy->fczjy", across_cos, spectrum[0]) - contract(
        "jx,fczxy->fczjy", across_sin, spectrum[1]
    )
    across_other = contract("jx,fczxy->fczjy", across_cos, spectrum[1]) + contract(
        "jx,fczxy->fczjy", across_sin, spectrum[0]
    )
    down_real = contract("my,fczjy->fczjm", down_cos, across_real) - contract(
        "my,fczjy->fczjm", down_sin, across_other
    )
    down_other = contract("my,fczjy->fczjm", down_cos, across_other) + contract(
        "my,fczjy->fczjm", down_sin, across_real
    )
    planes = jnp.stack([down_real, down_other]).astype(jnp.bfloat16)
    arrived = lax.all_to_all(planes, "slab", split_axis=5, concat_axis=3, tiled=True).astype(
        jnp.float32
    )
    depth_real = contract("wz,fczxy->fcxyw", depth_cos, arrived[0]) - contract(
        "wz,fczxy->fcxyw", depth_sin, arrived[1]
    )
    depth_other = contract("wz,fczxy->fcxyw", depth_cos, arrived[1]) + contract(
        "wz,fczxy->fcxyw", depth_sin, arrived[0]
    )
    sens_real = sens[0][None]
    sens_other = sens[1][None]
    combined_real = jnp.sum(sens_real * depth_real + sens_other * depth_other, axis=1)
    combined_other = jnp.sum(sens_real * depth_other - sens_other * depth_real, axis=1)
    matrix = jnp.stack([combined_real, combined_other], axis=1).reshape(frames_dev, -1)
    rows = lax.all_to_all(matrix, "tm", split_axis=1, concat_axis=0, tiled=True)
    gram = lax.psum(matmul(rows, rows.T), ("tm", "slab"))
    eye = jnp.eye(RANK, dtype=jnp.float32)
    current = jnp.concatenate([eye, eye], axis=1)
    for sweep_index in range(ITERS):
        current = matmul(orthonormal(current, gram), gram)
    coeff = orthonormal(current, gram)
    mixing = matmul(matmul(coeff, gram).T, coeff)
    projected = matmul(mixing, rows)
    projected = lax.all_to_all(projected, "tm", split_axis=0, concat_axis=1, tiled=True)
    return projected.reshape(frames_dev, 2, XW, -1, NZ)


def solution(mesh):
    in_specs = (P(None, "tm", None, "slab", None), P(None, None, None, "slab", None))
    out_specs = P("tm", None, None, "slab", None)
    return jax.shard_map(local, mesh=mesh, in_specs=in_specs, out_specs=out_specs, check_vma=False)
```

profile of v0, /device:TPU:0, one launch (start us, length us, event | category | flops | bytes accessed | tf_op | source)
XLA Modules:
  0.0 234.5 jit_solution(5598859404871233806)
XLA Ops:
  0.0 5.4 %fusion.180 = (bf16[1,2,4,24,9984]{4,3,2,1,0:T(8,128)(2,1)}, bf16[1,2,4,24,9984]{4,3,2,1,0:T(8,128)(2,1)}) fusion(bf16[2,2,4,24,9984]{4,3,2,1,0:T(8,128)(2,1)} %param.5), kind=kLoop, calls=%fused_computation.213 | loop fusion | bytes 15335424 | tf_op jit(solution)/shard_map/slice | solution.py:44
  5.4 13.7 %squeeze.16 = bf16[2,4,24,96,104]{4,3,2,1,0:T(8,128)(2,1)} reshape(bf16[1,2,4,24,9984]{4,3,2,1,0:T(8,128)(2,1)} %get-tuple-element.9) | data formatting | bytes 7667712 | tf_op jit(solution)/shard_map/squeeze | solution.py:44
  19.2 13.8 %squeeze.17 = bf16[2,4,24,96,104]{4,3,2,1,0:T(8,128)(2,1)} reshape(bf16[1,2,4,24,9984]{4,3,2,1,0:T(8,128)(2,1)} %get-tuple-element.10) | data formatting | bytes 7667712 | tf_op jit(solution)/shard_map/squeeze | solution.py:45
  33.0 4.3 %fusion.105 = f32[8,2,4,24,104]{4,0,3,2,1:T(8,128)S(1)} fusion(bf16[2,4,24,96,104]{4,3,2,1,0:T(8,128)(2,1)} %squeeze.16, s32[8]{0:T(128)S(1)} %iota_add_fusion), kind=kOutput, calls=%fused_computation.133 | convolution fusion | flops 184032768 | bytes 4472864 | tf_op jit(solution)/shard_map/jx,fczxy->fczjy/dot_general | solution.py:24
  37.3 2.1 fusion.103
  39.4 2.1 fusion.1
  41.4 1.0 fusion.10
  42.5 2.1 fusion
  44.5 1.0 fusion.6
  45.5 1.0 fusion.5
  46.5 1.0 fusion.4
  47.5 1.1 pad_maximum_fusion
  48.6 5.8 %copy.42 = bf16[2,2,4,24,8,104]{3,4,2,1,0,5:T(8,128)(2,1)S(1)} copy(bf16[2,2,4,24,8,104]{5,3,4,2,1,0:T(8,128)(2,1)} %pad_maximum_fusion) | data formatting | bytes 1277952 | tf_op jit(solution)/shard_map/stack | solution.py:56
  54.4 5.0 %reshape.64 = bf16[4,2,39936]{2,1,0:T(2,128)(2,1)} reshape(bf16[104,2,2,4,8,24]{5,4,3,2,1,0:T(8,128)(2,1)S(1)} %bitcast.164) | data formatting | bytes 1277952
  59.4 4.4 %all-to-all-start = ((bf16[4,2,39936]{2,1,0:T(2,128)(2,1)}), bf16[4,2,39936]{2,1,0:T(2,128)(2,1)}, u32[]{:S(2)}, u32[]{:S(2)}) async-start(bf16[4,2,39936]{2,1,0:T(2,128)(2,1)} %reshape.64), calls=%async_computation | async-start | bytes 1277952 | tf_op jit(solution)/shard_map/all_to_all | solution.py:57
  63.8 1.2 slice_bitcast_fusion.1
  65.0 0.9 copy.37
  65.9 0.9 copy.46
  66.8 8.7 %all-to-all-done = bf16[4,2,39936]{2,1,0:T(2,128)(2,1)} async-done(((bf16[4,2,39936]{2,1,0:T(2,128)(2,1)}), bf16[4,2,39936]{2,1,0:T(2,128)(2,1)}, u32[]{:S(2)}, u32[]{:S(2)}) %all-to-all-start) | async-done | bytes 639008 | tf_op jit(solution)/shard_map/all_to_all | solution.py:57
  75.5 5.6 %reshape.65 = bf16[104,2,2,4,8,24]{5,4,3,2,1,0:T(8,128)(2,1)S(1)} reshape(bf16[4,2,39936]{2,1,0:T(2,128)(2,1)} %all-to-all-done) | data formatting | bytes 1277952
  81.1 4.4 %copy.86 = bf16[2,2,4,24,8,4,26]{3,5,4,6,2,1,0:T(4,128)(2,1)S(1)} copy(bf16[2,2,4,24,8,4,26]{3,4,2,1,0,6,5:T(8,128)(2,1)S(1)} %bitcast.165) | data formatting | bytes 1277952 | tf_op jit(solution)/shard_map/all_to_all | solution.py:57
  85.5 1.2 fusion.181
  86.7 1.6 squeeze.18
  88.3 2.9 %fusion.16 = f32[2,4,8,26,96]{4,3,2,1,0:T(8,128)} fusion(bf16[2,4,96,8,26]{2,3,4,1,0:T(8,128)(2,1)} %squeeze.18), kind=kOutput, calls=%fused_computation.27 | convolution fusion | flops 184117248 | bytes 958464 | tf_op jit(solution)/shard_map/wz,fczxy->fcxyw/dot_general | solution.py:24
  91.1 0.9 squeeze.19
  92.0 0.8 fusion.12
  92.8 2.0 convolution_subtract_fusion
  94.9 2.2 add_reduce_fusion
  97.3 1.0 copy.49
  98.3 9.4 %all-to-all-start.1 = ((f32[2,32,1248]{2,0,1:T(2,128)}), f32[2,32,1248]{2,0,1:T(2,128)S(1)}, u32[]{:S(2)}, u32[]{:S(2)}) async-start(f32[2,32,1248]{2,0,1:T(2,128)} %copy.49), calls=%async_computation.1 | async-start | bytes 655360 | tf_op jit(solution)/shard_map/all_to_all | solution.py:71
  107.7 9.6 %all-to-all-done.1 = f32[2,32,1248]{2,0,1:T(2,128)S(1)} async-done(((f32[2,32,1248]{2,0,1:T(2,128)}), f32[2,32,1248]{2,0,1:T(2,128)S(1)}, u32[]{:S(2)}, u32[]{:S(2)}) %all-to-all-start.1) | async-done | bytes 319520 | tf_op jit(solution)/shard_map/all_to_all | solution.py:71
  117.8 0.4 fusion.182
  118.2 62.4 %psum.7 = f32[64,64]{1,0:T(8,128)S(1)} all-reduce(f32[64,64]{1,0:T(8,128)S(1)} %fusion.182), channel_id=1, replica_groups=mesh['tm'=32,'slab'=4] {'tm','slab'}, use_global_device_ids=true, to_apply=%region_2.3 | all-reduce | flops 4096 | bytes 32768 | tf_op jit(solution)/shard_map/psum | solution.py:72
  181.1 2.9 %cholesky.89 = f32[32,32]{1,0:T(8,128)S(1)} custom-call(f32[32,32]{1,0:T(8,128)S(1)} %fusion.89), custom_call_target="Cholesky" | custom-call | tf_op jit(solution)/shard_map/jit(cholesky)/cholesky | solution.py:32
  184.1 0.6 compare_reduce_fusion.4
  184.7 0.7 fusion.70
  185.4 2.4 %custom-call.9 = f32[1,32,32]{1,2,0:T(8,128)S(1)} custom-call(f32[1,32,32]{2,1,0:T(8,128)S(1)} %fusion.70), custom_call_target="InvertDiagBlocksLowerTriangular" | custom-call | tf_op jit(solution)/shard_map/triangular_solve/custom-call.0 | solution.py:33
  187.8 0.3 fusion.87
  188.6 2.9 %cholesky.100 = f32[32,32]{1,0:T(8,128)S(1)} custom-call(f32[32,32]{1,0:T(8,128)S(1)} %fusion.86), custom_call_target="Cholesky" | custom-call | tf_op jit(solution)/shard_map/jit(cholesky)/cholesky | solution.py:32
  191.6 0.6 compare_reduce_fusion.3
  192.2 0.7 fusion.71
  192.9 2.4 %custom-call.10 = f32[1,32,32]{1,2,0:T(8,128)S(1)} custom-call(f32[1,32,32]{2,1,0:T(8,128)S(1)} %fusion.71), custom_call_target="InvertDiagBlocksLowerTriangular" | custom-call | tf_op jit(solution)/shard_map/triangular_solve/custom-call.0 | solution.py:33
  195.3 0.2 fusion.84
  196.1 2.9 %cholesky.111 = f32[32,32]{1,0:T(8,128)S(1)} custom-call(f32[32,32]{1,0:T(8,128)S(1)} %fusion.83), custom_call_target="Cholesky" | custom-call | tf_op jit(solution)/shard_map/jit(cholesky)/cholesky | solution.py:32
  199.1 0.6 compare_reduce_fusion.2
  199.7 0.7 fusion.72
  200.4 2.4 %custom-call.11 = f32[1,32,32]{1,2,0:T(8,128)S(1)} custom-call(f32[1,32,32]{2,1,0:T(8,128)S(1)} %fusion.72), custom_call_target="InvertDiagBlocksLowerTriangular" | custom-call | tf_op jit(solution)/shard_map/triangular_solve/custom-call.0 | solution.py:33
  202.8 0.2 fusion.81
  203.6 2.9 %cholesky.122 = f32[32,32]{1,0:T(8,128)S(1)} custom-call(f32[32,32]{1,0:T(8,128)S(1)} %fusion.80), custom_call_target="Cholesky" | custom-call | tf_op jit(solution)/shard_map/jit(cholesky)/cholesky | solution.py:32
  206.5 0.6 compare_reduce_fusion.1
  207.2 0.7 fusion.73
  207.8 2.4 %custom-call.12 = f32[1,32,32]{1,2,0:T(8,128)S(1)} custom-call(f32[1,32,32]{2,1,0:T(8,128)S(1)} %fusion.73), custom_call_target="InvertDiagBlocksLowerTriangular" | custom-call | tf_op jit(solution)/shard_map/triangular_solve/custom-call.0 | solution.py:33
  210.3 0.2 fusion.78
  211.1 2.9 %cholesky.133 = f32[32,32]{1,0:T(8,128)S(1)} custom-call(f32[32,32]{1,0:T(8,128)S(1)} %fusion.77), custom_call_target="Cholesky" | custom-call | tf_op jit(solution)/shard_map/jit(cholesky)/cholesky | solution.py:32
  214.0 0.6 compare_reduce_fusion
  214.7 0.7 fusion.74
  215.3 2.4 %custom-call.13 = f32[1,32,32]{1,2,0:T(8,128)S(1)} custom-call(f32[1,32,32]{2,1,0:T(8,128)S(1)} %fusion.74), custom_call_target="InvertDiagBlocksLowerTriangular" | custom-call | tf_op jit(solution)/shard_map/triangular_solve/custom-call.0 | solution.py:33
  217.8 0.2 fusion.75
  218.2 0.2 fusion.196
  218.4 0.4 fusion.36
  218.8 0.3 copy.56
  219.1 14.0 %all_to_all.47 = f32[32,2,1248]{2,1,0:T(2,128)S(1)} all-to-all(f32[32,2,1248]{2,1,0:T(2,128)S(1)} %copy.56), channel_id=1, replica_groups=mesh['tm'=32,'slab'=4] {'tm'}, dimensions={0} | all-to-all | bytes 638976 | tf_op jit(solution)/shard_map/all_to_all | solution.py:80
  233.2 0.3 reshape.37
  233.4 1.0 copy.58
  (48 shorter events, 3.6 us)
Async XLA Ops:
  33.0 4.3 %copy-start = (bf16[2,4,24,96,104]{4,3,2,1,0:T(8,128)(2,1)S(1)}, bf16[2,4,24,96,104]{4,3,2,1,0:T(8,128)(2,1)}, u32[]{:S(2)}) copy-start(bf16[2,4,24,96,104]{4,3,2,1,0:T(8,128)(2,1)} %squeeze.17) | copy-start | bytes 11501572
  37.3 5.1 %slice-start = ((s8[4718592]{0:T(1024)(128)(4,1)}), s8[4194304]{0:T(1024)(128)(4,1)S(1)}, s32[]{:S(2)}) async-start(s8[4718592]{0:T(1024)(128)(4,1)} %bitcast.161), calls=%async_computation.3 | async-start | bytes 8388608
  39.4 3.1 %slice-start.1 = ((s8[4718592]{0:T(1024)(128)(4,1)}), s8[524288]{0:T(1024)(128)(4,1)S(1)}, s32[]{:S(2)}) async-start(s8[4718592]{0:T(1024)(128)(4,1)} %bitcast.161), calls=%async_computation.4 | async-start | bytes 1048576
  59.4 16.1 %all-to-all-start = ((bf16[4,2,39936]{2,1,0:T(2,128)(2,1)}), bf16[4,2,39936]{2,1,0:T(2,128)(2,1)}, u32[]{:S(2)}, u32[]{:S(2)}) async-start(bf16[4,2,39936]{2,1,0:T(2,128)(2,1)} %reshape.64), calls=%async_computation | async-start | bytes 1277952 | tf_op jit(solution)/shard_map/all_to_all | solution.py:57
  88.3 6.6 %copy-start.1 = (bf16[2,4,96,8,26]{2,3,4,1,0:T(8,128)(2,1)S(1)}, bf16[2,4,96,8,26]{2,3,4,1,0:T(8,128)(2,1)}, u32[]{:S(2)}) copy-start(bf16[2,4,96,8,26]{2,3,4,1,0:T(8,128)(2,1)} %squeeze.18) | copy-start | bytes 958468
  88.3 6.6 %copy-start.2 = (f32[4,8,26,96]{3,2,1,0:T(8,128)S(1)}, f32[4,8,26,96]{3,2,1,0:T(8,128)}, u32[]{:S(2)}) copy-start(f32[4,8,26,96]{3,2,1,0:T(8,128)} %copy.37) | copy-start | bytes 958468
  98.3 19.0 %all-to-all-start.1 = ((f32[2,32,1248]{2,0,1:T(2,128)}), f32[2,32,1248]{2,0,1:T(2,128)S(1)}, u32[]{:S(2)}, u32[]{:S(2)}) async-start(f32[2,32,1248]{2,0,1:T(2,128)} %copy.49), calls=%async_computation.1 | async-start | bytes 655360 | tf_op jit(solution)/shard_map/all_to_all | solution.py:71
where the time goes:
time: 235 us; the launch traced here: 234 us
  blocking collectives  76.4 us (33%)
  local copies, waits for them, and re-layouts  64.1 us (27%)
  other arithmetic  34.6 us (15%)
  matrix products  26.8 us (11%)
  waiting for transfers between devices  18.3 us (8%)
  starting transfers between devices  13.7 us (6%)
    psum x1, blocking collectives, local(): gram = lax.psum(matmul(rows, rows.T), ('tm', 'slab'))  62.4 us
    dot_general x12, matrix products, contract(): jnp.einsum(pattern, matrix_table, operand, precision=lax.Precision.HIGHEST)  22.3 us
    another operation x16, other arithmetic, orthonormal(): factor = jnp.linalg.cholesky(matmul(matmul(rows, gram), rows.T))  18 us
    another operation x10, other arithmetic, orthonormal(): return lax.linalg.triangular_solve(factor, rows, left_side=True, lower=True)  15.4 us
    all_to_all x1, blocking collectives, local(): lax.all_to_all(projected, 'tm', split_axis=0, concat_axis=1, tiled=True)  14 us
    squeeze x1, local copies, waits for them, and re-layouts, local(): spectrum[1]  13.8 us
    squeeze x1, local copies, waits for them, and re-layouts, local(): spectrum[0]  13.7 us
    unnamed x12, local copies, waits for them, and re-layouts  10.6 us
  transfers between devices with their start and end apart: 2, of which 2 were waited for; matrix products, arithmetic and copies ran while one was open for 1% of the time, Pallas kernels for 0%

commit v1 on v0

--- a/solution.py
+++ b/solution.py
@@ -69,7 +69,7 @@
     combined_other = jnp.sum(sens_real * depth_other - sens_other * depth_real, axis=1)
     matrix = jnp.stack([combined_real, combined_other], axis=1).reshape(frames_dev, -1)
     rows = lax.all_to_all(matrix, "tm", split_axis=1, concat_axis=0, tiled=True)
-    gram = lax.psum(matmul(rows, rows.T), ("tm", "slab"))
+    gram = lax.psum(lax.psum(matmul(rows, rows.T), "tm"), "slab")
     eye = jnp.eye(RANK, dtype=jnp.float32)
     current = jnp.concatenate([eye, eye], axis=1)
     for sweep_index in range(ITERS):

time: 235 us -> 340 us (1.45)
  blocking collectives: 76.4 us -> 181 us
    psum x1 -> x2, blocking collectives: 62.4 us -> 168 us  [local(): gram = lax.psum(lax.psum(matmul(rows, rows.T), 'tm'), 'slab')]
where the time goes in v1:
time: 340 us; the launch traced here: 339 us
  blocking collectives  181 us (53%)
  local copies, waits for them, and re-layouts  64.1 us (19%)
  other arithmetic  34.6 us (10%)
  matrix products  26.8 us (8%)
  waiting for transfers between devices  18.3 us (5%)
  starting transfers between devices  13.7 us (4%)
    psum x2, blocking collectives, local(): gram = lax.psum(lax.psum(matmul(rows, rows.T), 'tm'), 'slab')  168 us
    dot_general x12, matrix products, contract(): jnp.einsum(pattern, matrix_table, operand, precision=lax.Precision.HIGHEST)  22.3 us
    another operation x16, other arithmetic, orthonormal(): factor = jnp.linalg.cholesky(matmul(matmul(rows, gram), rows.T))  18 us
    another operation x10, other arithmetic, orthonormal(): return lax.linalg.triangular_solve(factor, rows, left_side=True, lower=True)  15.4 us
    squeeze x1, local copies, waits for them, and re-layouts, local(): spectrum[1]  13.8 us
    squeeze x1, local copies, waits for them, and re-layouts, local(): spectrum[0]  13.7 us
    all_to_all x1, blocking collectives, local(): lax.all_to_all(projected, 'tm', split_axis=0, concat_axis=1, tiled=True)  13.3 us
    unnamed x12, local copies, waits for them, and re-layouts  10.6 us
  transfers between devices with their start and end apart: 2, of which 2 were waited for; matrix products, arithmetic and copies ran while one was open for 1% of the time, Pallas kernels for 0%

profile of v1, /device:TPU:0, one launch (start us, length us, event | category | flops | bytes accessed | tf_op | source)
XLA Modules:
  0.0 339.2 jit_solution(6064368612708245236)
XLA Ops:
  0.0 5.4 %fusion.180 = (bf16[1,2,4,24,9984]{4,3,2,1,0:T(8,128)(2,1)}, bf16[1,2,4,24,9984]{4,3,2,1,0:T(8,128)(2,1)}) fusion(bf16[2,2,4,24,9984]{4,3,2,1,0:T(8,128)(2,1)} %param.5), kind=kLoop, calls=%fused_computation.213 | loop fusion | bytes 15335424 | tf_op jit(solution)/shard_map/slice | solution.py:44
  5.4 13.7 %squeeze.16 = bf16[2,4,24,96,104]{4,3,2,1,0:T(8,128)(2,1)} reshape(bf16[1,2,4,24,9984]{4,3,2,1,0:T(8,128)(2,1)} %get-tuple-element.9) | data formatting | bytes 7667712 | tf_op jit(solution)/shard_map/squeeze | solution.py:44
  19.2 13.8 %squeeze.17 = bf16[2,4,24,96,104]{4,3,2,1,0:T(8,128)(2,1)} reshape(bf16[1,2,4,24,9984]{4,3,2,1,0:T(8,128)(2,1)} %get-tuple-element.10) | data formatting | bytes 7667712 | tf_op jit(solution)/shard_map/squeeze | solution.py:45
  33.0 4.3 %fusion.105 = f32[8,2,4,24,104]{4,0,3,2,1:T(8,128)S(1)} fusion(bf16[2,4,24,96,104]{4,3,2,1,0:T(8,128)(2,1)} %squeeze.16, s32[8]{0:T(128)S(1)} %iota_add_fusion), kind=kOutput, calls=%fused_computation.133 | convolution fusion | flops 184032768 | bytes 4472864 | tf_op jit(solution)/shard_map/jx,fczxy->fczjy/dot_general | solution.py:24
  37.3 2.1 fusion.103
  39.4 2.1 fusion.1
  41.4 1.0 fusion.10
  42.5 2.1 fusion
  44.5 1.0 fusion.6
  45.5 1.0 fusion.5
  46.5 1.0 fusion.4
  47.5 1.1 pad_maximum_fusion
  48.6 5.8 %copy.42 = bf16[2,2,4,24,8,104]{3,4,2,1,0,5:T(8,128)(2,1)S(1)} copy(bf16[2,2,4,24,8,104]{5,3,4,2,1,0:T(8,128)(2,1)} %pad_maximum_fusion) | data formatting | bytes 1277952 | tf_op jit(solution)/shard_map/stack | solution.py:56
  54.4 5.0 %reshape.64 = bf16[4,2,39936]{2,1,0:T(2,128)(2,1)} reshape(bf16[104,2,2,4,8,24]{5,4,3,2,1,0:T(8,128)(2,1)S(1)} %bitcast.164) | data formatting | bytes 1277952
  59.4 4.4 %all-to-all-start = ((bf16[4,2,39936]{2,1,0:T(2,128)(2,1)}), bf16[4,2,39936]{2,1,0:T(2,128)(2,1)}, u32[]{:S(2)}, u32[]{:S(2)}) async-start(bf16[4,2,39936]{2,1,0:T(2,128)(2,1)} %reshape.64), calls=%async_computation | async-start | bytes 1277952 | tf_op jit(solution)/shard_map/all_to_all | solution.py:57
  63.8 1.2 slice_bitcast_fusion.1
  65.0 0.9 copy.37
  65.9 0.9 copy.46
  66.8 8.7 %all-to-all-done = bf16[4,2,39936]{2,1,0:T(2,128)(2,1)} async-done(((bf16[4,2,39936]{2,1,0:T(2,128)(2,1)}), bf16[4,2,39936]{2,1,0:T(2,128)(2,1)}, u32[]{:S(2)}, u32[]{:S(2)}) %all-to-all-start) | async-done | bytes 639008 | tf_op jit(solution)/shard_map/all_to_all | solution.py:57
  75.5 5.6 %reshape.65 = bf16[104,2,2,4,8,24]{5,4,3,2,1,0:T(8,128)(2,1)S(1)} reshape(bf16[4,2,39936]{2,1,0:T(2,128)(2,1)} %all-to-all-done) | data formatting | bytes 1277952
  81.1 4.4 %copy.86 = bf16[2,2,4,24,8,4,26]{3,5,4,6,2,1,0:T(4,128)(2,1)S(1)} copy(bf16[2,2,4,24,8,4,26]{3,4,2,1,0,6,5:T(8,128)(2,1)S(1)} %bitcast.165) | data formatting | bytes 1277952 | tf_op jit(solution)/shard_map/all_to_all | solution.py:57
  85.5 1.2 fusion.181
  86.7 1.6 squeeze.18
  88.3 2.9 fusion.16
  91.1 0.9 squeeze.19
  92.0 0.8 fusion.12
  92.8 2.0 convolution_subtract_fusion
  94.9 2.2 add_reduce_fusion
  97.3 1.0 copy.49
  98.3 9.4 %all-to-all-start.1 = ((f32[2,32,1248]{2,0,1:T(2,128)}), f32[2,32,1248]{2,0,1:T(2,128)S(1)}, u32[]{:S(2)}, u32[]{:S(2)}) async-start(f32[2,32,1248]{2,0,1:T(2,128)} %copy.49), calls=%async_computation.1 | async-start | bytes 655360 | tf_op jit(solution)/shard_map/all_to_all | solution.py:71
  107.7 9.6 %all-to-all-done.1 = f32[2,32,1248]{2,0,1:T(2,128)S(1)} async-done(((f32[2,32,1248]{2,0,1:T(2,128)}), f32[2,32,1248]{2,0,1:T(2,128)S(1)}, u32[]{:S(2)}, u32[]{:S(2)}) %all-to-all-start.1) | async-done | bytes 319520 | tf_op jit(solution)/shard_map/all_to_all | solution.py:71
  117.8 0.4 fusion.182
  118.2 154.7 %psum.14 = f32[64,64]{1,0:T(8,128)S(1)} all-reduce(f32[64,64]{1,0:T(8,128)S(1)} %fusion.182), channel_id=1, replica_groups=mesh['tm'=32,'slab'=4] {'tm'}, use_global_device_ids=true, to_apply=%region_2.3 | all-reduce | flops 4096 | bytes 32768 | tf_op jit(solution)/shard_map/psum | solution.py:72
  272.9 13.3 %psum.15 = f32[64,64]{1,0:T(8,128)S(1)} all-reduce(f32[64,64]{1,0:T(8,128)S(1)} %psum.14), channel_id=1, replica_groups=mesh['tm'=32,'slab'=4] {'slab'}, use_global_device_ids=true, to_apply=%region_3.4 | all-reduce | flops 4096 | bytes 32768 | tf_op jit(solution)/shard_map/psum | solution.py:72
  286.7 2.9 cholesky.89
  289.6 0.6 compare_reduce_fusion.4
  290.3 0.7 fusion.70
  290.9 2.4 custom-call.9
  293.4 0.3 fusion.87
  294.2 2.9 cholesky.100
  297.1 0.6 compare_reduce_fusion.3
  297.8 0.7 fusion.71
  298.4 2.4 custom-call.10
  300.9 0.2 fusion.84
  301.7 2.9 cholesky.111
  304.6 0.6 compare_reduce_fusion.2
  305.3 0.7 fusion.72
  305.9 2.4 custom-call.11
  308.4 0.2 fusion.81
  309.1 2.9 cholesky.122
  312.1 0.6 compare_reduce_fusion.1
  312.8 0.7 fusion.73
  313.4 2.4 custom-call.12
  315.8 0.2 fusion.78
  316.6 2.9 cholesky.133
  319.6 0.6 compare_reduce_fusion
  320.2 0.7 fusion.74
  320.9 2.4 custom-call.13
  323.7 0.2 fusion.196
  324.0 0.4 fusion.36
  324.4 0.3 copy.56
  324.7 13.3 %all_to_all.47 = f32[32,2,1248]{2,1,0:T(2,128)S(1)} all-to-all(f32[32,2,1248]{2,1,0:T(2,128)S(1)} %copy.56), channel_id=1, replica_groups=mesh['tm'=32,'slab'=4] {'tm'}, dimensions={0} | all-to-all | bytes 638976 | tf_op jit(solution)/shard_map/all_to_all | solution.py:80
  337.9 0.3 reshape.37
  338.2 1.0 copy.58
  (49 shorter events, 3.8 us)
Async XLA Ops:
  33.0 4.3 %copy-start = (bf16[2,4,24,96,104]{4,3,2,1,0:T(8,128)(2,1)S(1)}, bf16[2,4,24,96,104]{4,3,2,1,0:T(8,128)(2,1)}, u32[]{:S(2)}) copy-start(bf16[2,4,24,96,104]{4,3,2,1,0:T(8,128)(2,1)} %squeeze.17) | copy-start | bytes 11501572
  37.3 5.1 %slice-start = ((s8[4718592]{0:T(1024)(128)(4,1)}), s8[4194304]{0:T(1024)(128)(4,1)S(1)}, s32[]{:S(2)}) async-start(s8[4718592]{0:T(1024)(128)(4,1)} %bitcast.161), calls=%async_computation.3 | async-start | bytes 8388608
  39.4 3.1 slice-start.1
  59.4 16.1 %all-to-all-start = ((bf16[4,2,39936]{2,1,0:T(2,128)(2,1)}), bf16[4,2,39936]{2,1,0:T(2,128)(2,1)}, u32[]{:S(2)}, u32[]{:S(2)}) async-start(bf16[4,2,39936]{2,1,0:T(2,128)(2,1)} %reshape.64), calls=%async_computation | async-start | bytes 1277952 | tf_op jit(solution)/shard_map/all_to_all | solution.py:57
  88.3 6.6 %copy-start.1 = (bf16[2,4,96,8,26]{2,3,4,1,0:T(8,128)(2,1)S(1)}, bf16[2,4,96,8,26]{2,3,4,1,0:T(8,128)(2,1)}, u32[]{:S(2)}) copy-start(bf16[2,4,96,8,26]{2,3,4,1,0:T(8,128)(2,1)} %squeeze.18) | copy-start | bytes 958468
  88.3 6.6 %copy-start.2 = (f32[4,8,26,96]{3,2,1,0:T(8,128)S(1)}, f32[4,8,26,96]{3,2,1,0:T(8,128)}, u32[]{:S(2)}) copy-start(f32[4,8,26,96]{3,2,1,0:T(8,128)} %copy.37) | copy-start | bytes 958468
  98.3 19.0 %all-to-all-start.1 = ((f32[2,32,1248]{2,0,1:T(2,128)}), f32[2,32,1248]{2,0,1:T(2,128)S(1)}, u32[]{:S(2)}, u32[]{:S(2)}) async-start(f32[2,32,1248]{2,0,1:T(2,128)} %copy.49), calls=%async_computation.1 | async-start | bytes 655360 | tf_op jit(solution)/shard_map/all_to_all | solution.py:71
